TPU v7x, 32 devices: a whole 2x2x4 slice. The times are simulated.
32 devices in a mesh: req: 8 (over z, y), tp: 4 (over x, core).
Axes of the slice: x: 2, y: 2, z: 4, core: 2. Of those that a mesh axis runs over, the one named last changes fastest.
Arguments:
- tokens: bfloat16 [1024, 4096], P(('req', 'tp')), parts along dimension 0, may hold values from -400 to 400
- norm_gain: bfloat16 [4096], replicated, may hold values from 0.099609375 to 1.8984375
- qkv_weight: bfloat16 [4096, 1536], P(None, 'tp'), may hold values from -0.46875 to 0.46875
- out_weight: bfloat16 [512, 4096], P('tp'), may hold values from -0.5 to 0.5
- segment_ids: int32 [1024], P('req'), parts along dimension 0, may hold values from 0 to 7, never falling along the last dimension, each value on 1 to 42 neighbouring positions
- prefix_pages: int32 [64], P('req'), parts along dimension 0, may hold values from 1 to 16, 48 in all
- page_order: int32 [384], P('req'), parts along dimension 0, may hold values from 0 to 47, each once
- fresh_order: int32 [128], P('req'), parts along dimension 0, may hold values from 0 to 15, each once
- cache_pool: bfloat16 [2, 4, 384, 16, 128], P(None, 'tp', 'req'), parts along dimension 2, may hold values from -6 to 6
Outputs:
- attn_out: bfloat16 [1024, 4096], P(('req', 'tp')), parts along dimension 0
- fresh_pages: bfloat16 [2, 4, 128, 16, 128], P(None, 'tp', 'req'), parts along dimension 2
There are 8 independent parts, one for each index of `req`. A program takes and returns all parts, laid end to end along the dimension named above; an argument that names none is the same for every part. Nothing has to cross between parts.
Inputs may be any that keep to these rules, and one draw needn't show every extreme that they name: `segment_ids`: segment numbers never fall; every prompt has at least one new token and one has exactly 42. `prefix_pages`: they sum to 48; the largest is 16. `page_order`: every page once. `fresh_order`: every page once.
All inputs are finite; a program needn't handle non-finite values.
Results may differ from a plain program's by a relative error of at most 0.014.
Values may be sent and summed in bfloat16 or wider, within the bound.
A program may use at most 64 MiB of HBM per device.

v0:
```python
import jax
import jax.numpy as jnp
from jax import lax
from jax.sharding import PartitionSpec as P

MODEL_HEADS = 32


def layer_norm(values, gain):
    values = values.astype(jnp.float32)
    center = values - jnp.mean(values, axis=-1, keepdims=True)
    spread = jnp.mean(center * center, axis=-1, keepdims=True)
    return (center * lax.rsqrt(spread + 1e-05) * gain.astype(jnp.float32)).astype(jnp.bfloat16)


def token_layout(segment_ids, prefix_pages, page_order, fresh_order, page_len):
    seq_count = prefix_pages.shape[0]
    tok_count = segment_ids.shape[0]
    labels = jnp.arange(seq_count, dtype=jnp.int32)
    member = (segment_ids[:, None] == labels[None, :]).astype(jnp.int32)
    counts = jnp.sum(member, axis=0)
    starts = jnp.cumsum(counts) - counts
    token_index = jnp.arange(tok_count, dtype=jnp.int32)
    in_prompt = token_index - jnp.sum(member * starts[None, :], axis=1)
    prefix_len = prefix_pages * page_len
    position = in_prompt + jnp.sum(member * prefix_len[None, :], axis=1)
    fresh_counts = (counts + page_len - 1) // page_len
    fresh_starts = jnp.cumsum(fresh_counts) - fresh_counts
    page_slot = jnp.sum(member * fresh_starts[None, :], axis=1) + in_prompt // page_len
    target = jnp.take(fresh_order, page_slot) * page_len + in_prompt % page_len
    page_count = page_order.shape[0]
    cache_starts = jnp.cumsum(prefix_pages) - prefix_pages
    logical = (
        jnp.zeros((page_count,), jnp.int32)
        .at[page_order]
        .set(jnp.arange(page_count, dtype=jnp.int32))
    )
    holder = jnp.sum((logical[:, None] >= cache_starts[None, :]).astype(jnp.int32), axis=1) - 1
    holder_start = jnp.sum(
        (holder[:, None] == labels[None, :]).astype(jnp.int32) * cache_starts[None, :], axis=1
    )
    slot_index = jnp.arange(page_len, dtype=jnp.int32)
    key_owner = jnp.repeat(holder, page_len)
    key_pos = ((logical - holder_start)[:, None] * page_len + slot_index[None, :]).reshape(-1)
    return (in_prompt, position, target, key_owner, key_pos)


def attention_mask(segment_ids, in_prompt, position, key_owner, key_pos):
    cache_ok = segment_ids[:, None] == key_owner[None, :]
    new_ok = (segment_ids[:, None] == segment_ids[None, :]) & (
        in_prompt[None, :] <= in_prompt[:, None]
    )
    allowed = jnp.concatenate([cache_ok, new_ok], axis=1)
    key_all = jnp.concatenate([key_pos, position])
    distance = (position[:, None] - key_all[None, :]).astype(jnp.float32)
    return (allowed, distance)


def attend_head(queries, key_rows, values, alibi_slope, allowed, distance):
    scores = lax.dot_general(
        queries, key_rows, (((1,), (1,)), ((), ())), preferred_element_type=jnp.float32
    )
    scores = scores * queries.shape[1] ** (-0.5) - alibi_slope * distance
    scores = jnp.where(allowed, scores, -1e30)
    peak_score = jnp.max(scores, axis=1, keepdims=True)
    weights = jnp.exp(scores - peak_score)
    weights_bf = (weights / jnp.sum(weights, axis=1, keepdims=True)).astype(jnp.bfloat16)
    return jnp.dot(weights_bf, values, preferred_element_type=jnp.float32).astype(jnp.bfloat16)


def body(
    tokens,
    norm_gain,
    qkv_weight,
    out_weight,
    segment_ids,
    prefix_pages,
    page_order,
    fresh_order,
    cache_pool,
):
    head_dev = cache_pool.shape[1]
    page_len = cache_pool.shape[3]
    head_size = cache_pool.shape[4]
    tp_size = lax.axis_size("tp")
    first_head = lax.axis_index("tp") * head_dev
    projected = jnp.dot(
        layer_norm(lax.all_gather(tokens, "tp", axis=0, tiled=True), norm_gain),
        qkv_weight,
        preferred_element_type=jnp.float32,
    ).astype(jnp.bfloat16)
    tok_count = projected.shape[0]
    in_prompt, position, target, key_owner, key_pos = token_layout(
        segment_ids, prefix_pages, page_order, fresh_order, page_len
    )
    allowed, distance = attention_mask(segment_ids, in_prompt, position, key_owner, key_pos)
    per_head = projected.reshape(tok_count, head_dev, 3, head_size)
    step_heads = MODEL_HEADS // (head_dev * tp_size)
    alibi_slope = jnp.exp2(
        -8.0 * (first_head + 0 + 1).astype(jnp.float32) * step_heads / MODEL_HEADS
    )
    key_rows = jnp.concatenate([cache_pool[0, 0].reshape(-1, head_size), per_head[:, 0, 1]], axis=0)
    values = jnp.concatenate([cache_pool[1, 0].reshape(-1, head_size), per_head[:, 0, 2]], axis=0)
    contexts = attend_head(per_head[:, 0, 0], key_rows, values, alibi_slope, allowed, distance)
    summed = lax.psum_scatter(
        jnp.dot(contexts, out_weight, preferred_element_type=jnp.float32).astype(jnp.bfloat16),
        "tp",
        scatter_dimension=0,
        tiled=True,
    )
    fresh_total = fresh_order.shape[0]
    new_kv = per_head[:, :, 1:3].transpose(2, 1, 0, 3)
    fresh_pages = (
        jnp.zeros((2, head_dev, fresh_total * page_len, head_size), jnp.bfloat16)
        .at[:, :, target]
        .set(new_kv)
    )
    return (summed, fresh_pages.reshape(2, head_dev, fresh_total, page_len, head_size))


def solution(mesh):
    placed = (
        P(("req", "tp"), None),
        P(),
        P(None, "tp"),
        P("tp", None),
        P("req"),
        P("req"),
        P("req"),
        P("req"),
        P(None, "tp", "req", None, None),
    )
    return jax.shard_map(
        body,
        mesh=mesh,
        in_specs=placed,
        out_specs=(P(("req", "tp"), None), P(None, "tp", "req", None, None)),
        check_vma=False,
    )
```

profile of v0, /device:TPU:0, one launch (start us, length us, event | category | flops | bytes accessed | tf_op | source)
XLA Modules:
  0.0 70.8 jit_solution(16435885710828232810)
XLA Ops:
  7.2 0.7 all-gather.2.cloned.1.call-update
  8.0 0.9 %convert_reduce_fusion.1 = s32[8]{0:T(128)S(1)} fusion(s32[128]{0:T(128)} %param.13), kind=kLoop, calls=%fused_computation.40 | loop fusion | flops 3064 | bytes 544 | tf_op jit(solution)/shard_map/reduce_sum | solution.py:21
  8.9 0.2 reduce-window.27
  9.1 0.2 reduce-window.26
  9.3 0.8 %reduce-window.25 = s32[8,1]{0,1:T(1,128)S(1)} reduce-window(s32[8,1]{0,1:T(1,128)} %bitcast.215, s32[]{:T(128)} %constant.87.clone.1), window={size=8x1 pad=7_0x0_0}, to_apply=%region_1.0 | reduce-window | flops 56 | bytes 68 | tf_op jit(solution)/shard_map/reduce-window.10
  10.1 0.7 compare_select_fusion.2
  10.8 0.7 %scatter_custom_fusion = s32[48]{0:T(128)S(1)} fusion(s32[48]{0:T(128)S(1)} %compare_select_fusion.2, s32[48]{0:T(128)S(1)} %iota.25, s32[]{:T(128)} %constant.87.clone.1), kind=kCustom, calls=%fused_computation.91 | custom fusion | bytes 196 | tf_op jit(solution)/shard_map/scatter | solution.py:36
  11.5 0.7 bitcast_subtract_fusion.2
  12.2 0.1 select_reduce_fusion.1
  12.5 0.7 convert_element_type.37
  13.4 1.3 %select_reduce_fusion = (s32[128]{0:T(128)}, s32[128]{0:T(128)S(1)}, s32[128]{0:T(128)S(1)}) fusion(s32[8]{0:T(128)S(1)} %get-tuple-element.36, s32[128]{0:T(128)} %param.13, s32[8]{0:T(128)S(1)} %get-tuple-element.39, s32[8]{0:T(128)S(1)} %get-tuple-element.35), kind=kLoop, calls=%fused_computation.35 | loop fusion | flops 6784 | bytes 2144 | tf_op jit(solution)/shard_map/reduce_sum | solution.py:29
  14.7 0.6 pad_add_fusion
  15.3 0.8 %compare_and_fusion = pred[128,128]{1,0:T(32,128)(4,1)S(1)} fusion(s32[128]{0:T(128)S(1)} %get-tuple-element.32, s32[128]{0:T(128)} %param.13), kind=kLoop, calls=%fused_computation.31 | loop fusion | flops 49152 | bytes 17408 | tf_op jit(solution)/shard_map/and | solution.py:50
  16.2 1.4 %broadcast_compare_fusion = pred[128,768]{1,0:T(32,128)(4,1)} fusion(s32[768]{0:T(1024)S(1)} %eq.29, s32[128]{0:T(128)} %param.13), kind=kLoop, calls=%fused_computation.29 | loop fusion | flops 98304 | bytes 101888 | tf_op jit(solution)/shard_map/eq | solution.py:49
  17.6 1.7 %fusion.36 = (bf16[1,1,48,16,128]{4,3,2,1,0:T(8,128)(2,1)S(1)}, bf16[1,1,48,16,128]{4,3,2,1,0:T(8,128)(2,1)}) fusion(bf16[2,1,48,16,128]{4,3,2,1,0:T(8,128)(2,1)} %param.17), kind=kLoop, calls=%fused_computation.96 | loop fusion | bytes 786432 | tf_op jit(solution)/shard_map/slice | solution.py:103
  19.3 9.7 %all-gather.2.cloned.1.call-done = bf16[128,4096]{1,0:T(8,128)(2,1)} async-done(((bf16[32,4096]{1,0:T(8,128)(2,1)}), bf16[128,4096]{1,0:T(8,128)(2,1)}) %all-gather.2.cloned.1.call-update) | async-done | bytes 1048592 | tf_op jit(solution)/shard_map/all_gather | solution.py:88
  29.0 1.5 %convert_reduce_fusion = f32[128]{0:T(128)S(1)} fusion(bf16[128,4096]{1,0:T(8,128)(2,1)} %all-gather.2.cloned.1.call-done), kind=kLoop, calls=%fused_computation.4 | loop fusion | flops 1048448 | bytes 1049088 | tf_op jit(solution)/shard_map/reduce_sum | solution.py:11
  30.6 1.7 %fusion.2 = f32[128]{0:T(128)S(1)} fusion(bf16[128,4096]{1,0:T(8,128)(2,1)} %all-gather.2.cloned.1.call-done, f32[128]{0:T(128)S(1)} %broadcast_multiply_fusion.1), kind=kLoop, calls=%fused_computation.7 | loop fusion | flops 2097024 | bytes 1049600 | tf_op jit(solution)/shard_map/reduce_sum | solution.py:12
  32.3 0.8 %convolution_convert_fusion.1 = bf16[128,384]{1,0:T(8,128)(2,1)S(1)} fusion(bf16[4096,384]{1,0:T(8,128)(2,1)S(1)} %copy-done, bf16[128,4096]{1,0:T(8,128)(2,1)S(1)} %copy-done.1, f32[4096]{0:T(1024)S(1)} %convert_element_type.37, f32[128]{0:T(128)S(1)} %add_rsqrt_fusion, f32[128]{0:T(128)S(1)} %broadcast_multiply_fusion.1), kind=kOutput, calls=%fused_computation.13 | convolution fusion | flops 405323776 | bytes 4310016 | tf_op jit(solution)/shard_map/dot_general | solution.py:87
  33.1 0.1 copy.18
  33.2 0.1 copy.20
  33.3 0.1 copy.21
  33.4 1.4 %fusion.39 = (f32[128]{0:T(128)S(1)}, f32[128,896]{1,0:T(8,128)S(1)}) fusion(s32[896]{0:T(1024)} %pad_add_fusion, s32[128]{0:T(128)} %copy-done.7, f32[]{:T(128)S(6)} %exp2.7, bf16[128,128]{1,0:T(8,128)(2,1)S(1)} %bitcast.214, bf16[768,128]{1,0:T(8,128)(2,1)} %bitcast.212, bf16[128,1,3,128]{0,3,2,1:T(8,128)(2,1)S(1)} %bitcast.209, ...), kind=kOutput, calls=%fused_computation.99 | convolution fusion | flops 30736256 | bytes 840196 | tf_op jit(solution)/shard_map/dot_general | solution.py:60
  34.8 0.8 %copy-done.2 = f32[128,896]{1,0:T(8,128)} copy-done((f32[128,896]{1,0:T(8,128)}, f32[128,896]{1,0:T(8,128)S(1)}, u32[]{:S(2)}) %copy-start.2) | copy-done | bytes 458776
  35.6 0.2 fusion.11
  35.8 3.1 %convolution_convert_fusion = bf16[128,4096]{1,0:T(8,128)(2,1)} fusion(bf16[128,4096]{1,0:T(8,128)(2,1)} %param.12, f32[128,896]{1,0:T(8,128)} %copy-done.2, bf16[128,128]{1,0:T(8,128)(2,1)S(1)} %bitcast.213, bf16[768,128]{1,0:T(8,128)(2,1)S(1)} %bitcast.211, f32[128]{0:T(128)S(1)} %fusion.11, f32[128]{0:T(128)S(1)} %get-tuple-element.37), kind=kOutput, calls=%fused_computation.2 | convolution fusion | flops 164921344 | bytes 2786304 | tf_op jit(solution)/shard_map/dot_general | solution.py:106
  38.9 0.7 %fusion.38 = (s32[1]{0:T(128)}, s32[1]{0:T(128)}, s32[1]{0:T(128)}, s32[1]{0:T(128)}, s32[1]{0:T(128)}, /*index=5*/s32[1]{0:T(128)}, s32[1]{0:T(128)}, s32[1]{0:...) fusion(s32[16]{0:T(128)S(1)} %copy-done.3), kind=kLoop, calls=%fused_computation.98 | loop fusion | bytes 128 | tf_op jit(solution)/shard_map/jit(_take)/gather | solution.py:30
  39.7 10.0 %fusion.29 = s32[128]{0:T(128)S(1)} fusion(s32[128]{0:T(128)S(1)} %copy-done.5, s32[128]{0:T(128)S(1)} %copy-done.6, s32[]{:T(128)} %bitcast.31, s32[]{:T(128)} %bitcast.32, s32[]{:T(128)} %bitcast.33, s32[]{:T(128)} %bitcast.34, s32[]{:T(128)} %bitcast.35, s32[]{:T(128)} %bitcast.37, s32[]{:T(128)} %bitcast.36, s32[]{:T(128)} %bitcast.14, s32[]{:T(128)} %bitcast.16, ...), kind=kLoop, calls=%fused_computation.79 | loop fusion | flops 8064 | bytes 1600 | tf_op jit(solution)/shard_map/select_n | solution.py:116
  49.6 0.1 copy.22
  49.9 4.4 %scatter_fusion = bf16[2,256,128]{2,0,1:T(2,128)(2,1)S(1)} fusion(bf16[2,256,128]{2,0,1:T(2,128)(2,1)S(1)} %broadcast.406, s32[128]{0:T(128)S(1)} %fusion.29, bf16[128,2,128]{2,1,0:T(2,128)(2,1)S(1)} %copy.22), kind=kCustom, calls=%fused_computation.1 | custom fusion | bytes 197120 | tf_op jit(solution)/shard_map/scatter | solution.py:116
  54.3 0.7 copy.23
  55.0 9.0 %reduce-scatter.2.cloned.1.call-done = bf16[32,4096]{1,0:T(8,128)(2,1)} async-done(((bf16[128,4096]{1,0:T(8,128)(2,1)}), bf16[32,4096]{1,0:T(8,128)(2,1)}) %reduce-scatter.2.cloned.1.call-update) | async-done | bytes 262160 | tf_op jit(solution)/shard_map/reduce_scatter | solution.py:105
  (33 shorter events, 0.7 us)
Async XLA Ops:
  7.2 25.1 %copy-start = (bf16[4096,384]{1,0:T(8,128)(2,1)S(1)}, bf16[4096,384]{1,0:T(8,128)(2,1)}, u32[]{:S(2)}) copy-start(bf16[4096,384]{1,0:T(8,128)(2,1)} %param.11) | copy-start | bytes 9437188
  7.2 21.8 %all-gather.2.cloned.1.call-start = ((), (), s32[]{:S(2)}) async-start(), calls=%async_computation.1 | async-start | bytes 1310720 | tf_op jit(solution)/shard_map/all_gather | solution.py:88
  7.9 56.1 %reduce-scatter.2.cloned.1.call-start = ((), (), s32[]{:S(2)}) async-start(), calls=%async_computation.2 | async-start | bytes 1310720 | tf_op jit(solution)/shard_map/reduce_scatter | solution.py:105
  14.7 1.4 %copy-start.4 = (s32[128]{0:T(128)}, s32[128]{0:T(128)S(1)}, u32[]{:S(2)}) copy-start(s32[128]{0:T(128)S(1)} %get-tuple-element.10) | copy-start | bytes 1540
  14.7 1.4 %copy-start.7 = (s32[128]{0:T(128)}, s32[128]{0:T(128)S(1)}, u32[]{:S(2)}) copy-start(s32[128]{0:T(128)S(1)} %get-tuple-element.31) | copy-start | bytes 1540
  29.0 3.2 %copy-start.1 = (bf16[128,4096]{1,0:T(8,128)(2,1)S(1)}, bf16[128,4096]{1,0:T(8,128)(2,1)}, u32[]{:S(2)}) copy-start(bf16[128,4096]{1,0:T(8,128)(2,1)} %all-gather.2.cloned.1.call-done) | copy-start | bytes 3145732
  34.8 0.8 %copy-start.2 = (f32[128,896]{1,0:T(8,128)}, f32[128,896]{1,0:T(8,128)S(1)}, u32[]{:S(2)}) copy-start(f32[128,896]{1,0:T(8,128)S(1)} %get-tuple-element.38) | copy-start | bytes 1376260
  35.8 3.1 %copy-start.3 = (s32[16]{0:T(128)S(1)}, s32[16]{0:T(128)}, u32[]{:S(2)}) copy-start(s32[16]{0:T(128)} %param.16) | copy-start | bytes 196
  35.8 3.8 %copy-start.5 = (s32[128]{0:T(128)S(1)}, s32[128]{0:T(128)}, u32[]{:S(2)}) copy-start(s32[128]{0:T(128)} %copy-done.4) | copy-start | bytes 1540
  35.8 3.8 %copy-start.6 = (s32[128]{0:T(128)S(1)}, s32[128]{0:T(128)}, u32[]{:S(2)}) copy-start(s32[128]{0:T(128)} %get-tuple-element.8) | copy-start | bytes 1540
Sparse Core Ops, SparseCore 0:
  9.6 19.4 all-gather.1
  39.0 24.8 reduce-scatter.1
where the time goes:
time: 71.3 us; the launch traced here: 70.8 us
  other arithmetic  22 us (31%)
  waiting for transfers between devices  19.4 us (27%)
  between operations  14.3 us (20%)
  local copies, waits for them, and re-layouts  9.89 us (14%)
  matrix products  5.2 us (7%)
    select_n x1, other arithmetic, body(): fresh_pages = jnp.zeros((2, head_dev, fresh_total * page_len, head_size),...  9.98 us
    all_gather x1, waiting for transfers between devices, body(): lax.all_gather(tokens, 'tp', axis=0, tiled=True)  9.69 us
    reduce_scatter x1, waiting for transfers between devices, body(): lax.psum_scatter(jnp.dot(contexts, out_weight, preferred_element_type=jnp...  9 us
    scatter x1, local copies, waits for them, and re-layouts, body(): fresh_pages = jnp.zeros((2, head_dev, fresh_total * page_len, head_size),...  4.42 us
    dot_general x1, matrix products, body(): jnp.dot(contexts, out_weight, preferred_element_type=jnp.float32)  3.06 us
    slice x1, local copies, waits for them, and re-layouts, body(): cache_pool[1, 0].reshape(-1, head_size)  1.74 us
    reduce_sum x1, other arithmetic, layer_norm(): spread = jnp.mean(center * center, axis=-1, keepdims=True)  1.65 us
    reduce_sum x1, other arithmetic, layer_norm(): center = values - jnp.mean(values, axis=-1, keepdims=True)  1.54 us
  transfers between devices with their start and end apart: 2, of which 2 were waited for; matrix products, arithmetic and copies ran while one was open for 39% of the time, Pallas kernels for 0%

commit v1 on v0

v1 whole, which is shorter than its diff:
```python
import functools
import jax
import jax.numpy as jnp
from jax import lax
from jax.experimental import pallas as pl
from jax.experimental.pallas import tpu as pltpu
from jax.sharding import PartitionSpec as P

MODEL_HEADS = 32
K_PARTS = 8
N_PARTS = 8
F32 = jnp.float32
BF16 = jnp.bfloat16


def iota(shape, dim):
    return lax.broadcasted_iota(jnp.int32, shape, dim).astype(F32)


def to_col(row):
    size = row.shape[1]
    eye = iota((size, size), 0) == iota((size, size), 1)
    return jnp.sum(jnp.where(eye, row, 0.0), axis=1, keepdims=True)


def kernel(
    n,
    page_len,
    tok_ref,
    gain_ref,
    seg_ref,
    prefix_ref,
    order_ref,
    fresh_ref,
    w_hbm,
    wo_hbm,
    cache_hbm,
    out_ref,
    pages_ref,
    xg,
    w_v,
    wo_v,
    cache_v,
    bias_c,
    bias_n,
    ctx_own,
    ctx_sib,
    stage,
    land,
    own_sum,
    w_sem,
    wo_sem,
    cache_sem,
    cross_send,
    cross_recv,
    sib_send,
    sib_recv,
    wo_send,
    wo_recv,
    ctx_send,
    ctx_recv,
    sum_send,
    sum_recv,
):
    m = n // 2
    me = lax.axis_index("tp")
    chip, core = me // 2, lax.rem(me, 2)
    sibling = chip * 2 + (1 - core)
    rows, width = tok_ref.shape
    toks = n * rows
    head = wo_hbm.shape[0]
    kc, nc = width // K_PARTS, width // N_PARTS

    def peer(d):
        return lax.rem(chip + d, m) * 2 + core

    def at_rows(owner):
        return pl.ds(pl.multiple_of(owner * rows, rows), rows)

    cache_copy = pltpu.make_async_copy(cache_hbm, cache_v, cache_sem)
    wo_copy = pltpu.make_async_copy(wo_hbm, wo_v.at[pl.ds(0, head)], wo_sem)
    w_copies = [
        pltpu.make_async_copy(
            w_hbm.at[pl.ds(j * kc, kc)], w_v.at[pl.ds(j * kc, kc)], w_sem.at[j]
        )
        for j in range(K_PARTS)
    ]

    def cross(j, d):
        block = xg.at[j, at_rows(me)]
        return pltpu.make_async_remote_copy(
            src_ref=block,
            dst_ref=block,
            send_sem=cross_send.at[j, d - 1],
            recv_sem=cross_recv.at[j, d - 1],
            device_id={"tp": peer(d)},
            device_id_type=pl.DeviceIdType.MESH,
        )

    def forward(j, d):
        block = xg.at[j, at_rows(peer(m - d))]
        return pltpu.make_async_remote_copy(
            src_ref=block,
            dst_ref=block,
            send_sem=sib_send.at[j, d],
            recv_sem=sib_recv.at[j, d],
            device_id={"tp": sibling},
            device_id_type=pl.DeviceIdType.MESH,
        )

    wo_push = pltpu.make_async_remote_copy(
        src_ref=wo_hbm,
        dst_ref=wo_v.at[pl.ds(head, head)],
        send_sem=wo_send,
        recv_sem=wo_recv,
        device_id={"tp": sibling},
        device_id_type=pl.DeviceIdType.MESH,
    )
    ctx_push = pltpu.make_async_remote_copy(
        src_ref=ctx_own,
        dst_ref=ctx_sib,
        send_sem=ctx_send,
        recv_sem=ctx_recv,
        device_id={"tp": sibling},
        device_id_type=pl.DeviceIdType.MESH,
    )

    def give(j, d):
        return pltpu.make_async_remote_copy(
            src_ref=stage.at[d - 1, j],
            dst_ref=land.at[d - 1, j],
            send_sem=sum_send.at[d - 1, j],
            recv_sem=sum_recv.at[d - 1, j],
            device_id={"tp": peer(d)},
            device_id_type=pl.DeviceIdType.MESH,
        )

    barrier = pltpu.get_barrier_semaphore()
    for other in [sibling] + [peer(d) for d in range(1, m)]:
        pl.semaphore_signal(
            barrier, inc=1, device_id={"tp": other}, device_id_type=pl.DeviceIdType.MESH
        )
    for copy in w_copies:
        copy.start()
    cache_copy.start()
    wo_copy.start()

    values = tok_ref[...].astype(F32)
    mean = jnp.sum(values, axis=1, keepdims=True) * (1.0 / width)
    center = values - mean
    spread = jnp.sum(center * center, axis=1, keepdims=True) * (1.0 / width)
    scale = lax.rsqrt(spread + 1e-05)
    pl.semaphore_wait(barrier, m)
    for j in range(K_PARTS):
        part = slice(j * kc, (j + 1) * kc)
        piece = (tok_ref[:, part].astype(F32) - mean) * scale * gain_ref[:, part].astype(F32)
        xg[j, at_rows(me), :] = piece.astype(BF16)
        for d in range(1, m):
            cross(j, d).start()
        forward(j, 0).start()
    wo_push.start()

    seqs = prefix_ref.shape[1]
    seg_row = seg_ref[...].astype(F32)
    prefix_row = prefix_ref[...].astype(F32)
    labels = iota((seqs, toks), 0)
    member = labels == seg_row
    before = labels < seg_row
    counts = jnp.sum(jnp.where(member, 1.0, 0.0), axis=1, keepdims=True)
    starts = jnp.sum(jnp.where(before, counts, 0.0), axis=0, keepdims=True)
    inside = iota((1, toks), 1) - starts
    page_inside = jnp.floor((inside + 0.5) * (1.0 / page_len))
    fresh_counts = jnp.floor((counts + (page_len - 0.5)) * (1.0 / page_len))
    page_slot = jnp.sum(jnp.where(before, fresh_counts, 0.0), axis=0, keepdims=True) + page_inside
    fresh_col = to_col(fresh_ref[...].astype(F32))
    fresh_total = fresh_col.shape[0]
    target = jnp.sum(
        jnp.where(iota((fresh_total, toks), 0) == page_slot, fresh_col, 0.0), axis=0, keepdims=True
    )
    target = target * page_len + (inside - page_inside * page_len)
    prefix_col = to_col(prefix_row)
    pos_row = inside + page_len * jnp.sum(
        jnp.where(member, prefix_col, 0.0), axis=0, keepdims=True
    )
    seg_col = to_col(seg_row)
    pos_col = to_col(pos_row)
    cache_starts = jnp.sum(
        jnp.where(iota((seqs, seqs), 1) < iota((seqs, seqs), 0), prefix_row, 0.0),
        axis=1,
        keepdims=True,
    )
    order_col = to_col(order_ref[...].astype(F32))
    pages = order_col.shape[0]
    cached = pages * page_len
    slot = iota((1, cached), 1)
    page_id = jnp.floor((slot + 0.5) * (1.0 / page_len))
    logical = jnp.sum(
        jnp.where(order_col == page_id, iota((pages, cached), 0), 0.0), axis=0, keepdims=True
    )
    reached = logical >= cache_starts
    holder = jnp.sum(jnp.where(reached, 1.0, 0.0), axis=0, keepdims=True) - 1.0
    holder_start = jnp.max(jnp.where(reached, cache_starts, 0.0), axis=0, keepdims=True)
    key_pos = (logical - holder_start) * page_len + (slot - page_id * page_len)
    step_heads = MODEL_HEADS // n
    slope = jnp.float32(2.0 ** (-8.0 * step_heads / MODEL_HEADS))
    for h in range(1, n):
        slope = jnp.where(me == h, jnp.float32(2.0 ** (-8.0 * (h + 1) * step_heads / MODEL_HEADS)), slope)
    bias_c[...] = jnp.where(seg_col == holder, (key_pos - pos_col) * slope, -1e30)
    causal = iota((toks, toks), 1) <= iota((toks, toks), 0)
    bias_n[...] = jnp.where((seg_col == seg_row) & causal, (pos_row - pos_col) * slope, -1e30)

    def project(j, total):
        for d in range(m):
            forward(j, d).wait_recv()
        w_copies[j].wait()
        product = jnp.dot(xg[j], w_v[pl.ds(j * kc, kc), :], preferred_element_type=F32)
        return product if total is None else total + product

    total = None
    for j in range(K_PARTS):
        for d in range(1, m):
            cross(j, d).wait_recv()
            forward(j, d).start()
        if j:
            total = project(j - 1, total)
    total = project(K_PARTS - 1, total)
    projected = total.astype(BF16)
    queries = projected[:, :head]
    key_new = projected[:, head : 2 * head]
    value_new = projected[:, 2 * head :]

    cache_copy.wait()
    contract = (((1,), (1,)), ((), ()))
    norm = head ** (-0.5)
    score_c = lax.dot_general(queries, cache_v[0], contract, preferred_element_type=F32)
    score_n = lax.dot_general(queries, key_new, contract, preferred_element_type=F32)
    score_c = score_c * norm + bias_c[...]
    score_n = score_n * norm + bias_n[...]
    peak = jnp.maximum(
        jnp.max(score_c, axis=1, keepdims=True), jnp.max(score_n, axis=1, keepdims=True)
    )
    weight_c = jnp.exp(score_c - peak)
    weight_n = jnp.exp(score_n - peak)
    mass = jnp.sum(weight_c, axis=1, keepdims=True) + jnp.sum(weight_n, axis=1, keepdims=True)
    context = jnp.dot(weight_c.astype(BF16), cache_v[1], preferred_element_type=F32)
    context = context + jnp.dot(weight_n.astype(BF16), value_new, preferred_element_type=F32)
    ctx_own[...] = (context / mass).astype(BF16)
    ctx_push.start()

    spots = iota((fresh_total * page_len, toks), 0) == target
    placed = jnp.dot(
        jnp.where(spots, 1.0, 0.0).astype(BF16), projected[:, head:], preferred_element_type=F32
    ).astype(BF16)
    pages_ref[0] = placed[:, :head]
    pages_ref[1] = placed[:, head:]

    wo_copy.wait()
    wo_push.wait_recv()
    ctx_push.wait_recv()
    order = list(range(1, m)) + [0]
    left = jnp.concatenate(
        [
            jnp.concatenate([ctx_own[at_rows(peer(d)), :] for d in order], axis=0),
            jnp.concatenate([ctx_sib[at_rows(peer(d)), :] for d in order], axis=0),
        ],
        axis=1,
    )
    for j in range(N_PARTS):
        part = slice(j * nc, (j + 1) * nc)
        product = jnp.dot(left, wo_v[:, part], preferred_element_type=F32)
        for d in range(1, m):
            stage[d - 1, j] = product[(d - 1) * rows : d * rows].astype(BF16)
            give(j, d).start()
        own_sum[:, part] = product[(m - 1) * rows :]
    for j in range(N_PARTS):
        part = slice(j * nc, (j + 1) * nc)
        whole = own_sum[:, part]
        for d in range(1, m):
            give(j, d).wait_recv()
            whole = whole + land[d - 1, j].astype(F32)
        out_ref[:, part] = whole.astype(BF16)

    for j in range(K_PARTS):
        for d in range(1, m):
            cross(j, d).wait_send()
        for d in range(m):
            forward(j, d).wait_send()
    wo_push.wait_send()
    ctx_push.wait_send()
    for j in range(N_PARTS):
        for d in range(1, m):
            give(j, d).wait_send()


def body(
    tokens,
    norm_gain,
    qkv_weight,
    out_weight,
    segment_ids,
    prefix_pages,
    page_order,
    fresh_order,
    cache_pool,
):
    n = lax.axis_size("tp")
    m = n // 2
    rows, width = tokens.shape
    toks = n * rows
    head_dev, pages, page_len, head = cache_pool.shape[1:]
    cached = pages * page_len
    fresh_total = fresh_order.shape[0]
    vmem = pl.BlockSpec(memory_space=pltpu.VMEM)
    hbm = pl.BlockSpec(memory_space=pl.ANY)
    dma = pltpu.SemaphoreType.DMA
    kc, nc = width // K_PARTS, width // N_PARTS
    attn_out, fresh_pages = pl.pallas_call(
        functools.partial(kernel, n, page_len),
        out_shape=(
            jax.ShapeDtypeStruct((rows, width), BF16),
            jax.ShapeDtypeStruct((2, fresh_total * page_len, head), BF16),
        ),
        in_specs=[vmem] * 6 + [hbm] * 3,
        out_specs=(vmem, vmem),
        scratch_shapes=[
            pltpu.VMEM((K_PARTS, toks, kc), BF16),
            pltpu.VMEM((width, 3 * head), BF16),
            pltpu.VMEM((2 * head, width), BF16),
            pltpu.VMEM((2, cached, head), BF16),
            pltpu.VMEM((toks, cached), F32),
            pltpu.VMEM((toks, toks), F32),
            pltpu.VMEM((toks, head), BF16),
            pltpu.VMEM((toks, head), BF16),
            pltpu.VMEM((m - 1, N_PARTS, rows, nc), BF16),
            pltpu.VMEM((m - 1, N_PARTS, rows, nc), BF16),
            pltpu.VMEM((rows, width), F32),
            dma((K_PARTS,)),
            dma,
            dma,
            dma((K_PARTS, m - 1)),
            dma((K_PARTS, m - 1)),
            dma((K_PARTS, m)),
            dma((K_PARTS, m)),
            dma,
            dma,
            dma,
            dma,
            dma((m - 1, N_PARTS)),
            dma((m - 1, N_PARTS)),
        ],
        compiler_params=pltpu.CompilerParams(
            collective_id=0, has_side_effects=True, vmem_limit_bytes=56 * 1024 * 1024
        ),
    )(
        tokens,
        norm_gain.reshape(1, -1),
        segment_ids.reshape(1, -1),
        prefix_pages.reshape(1, -1),
        page_order.reshape(1, -1),
        fresh_order.reshape(1, -1),
        qkv_weight,
        out_weight,
        cache_pool.reshape(2, cached, head),
    )
    return attn_out, fresh_pages.reshape(2, head_dev, fresh_total, page_len, head)


def solution(mesh):
    placed = (
        P(("req", "tp"), None),
        P(),
        P(None, "tp"),
        P("tp", None),
        P("req"),
        P("req"),
        P("req"),
        P("req"),
        P(None, "tp", "req", None, None),
    )
    return jax.shard_map(
        body,
        mesh=mesh,
        in_specs=placed,
        out_specs=(P(("req", "tp"), None), P(None, "tp", "req", None, None)),
        check_vma=False,
    )
```

time: 71.3 us -> 29 us (0.41)
  Pallas kernels: 0 us -> 23.5 us
  other arithmetic: 22 us -> 0 us
  waiting for transfers between devices: 19.4 us -> 0 us
  between operations: 14.3 us -> 0.64 us
  local copies, waits for them, and re-layouts: 9.89 us -> 4.55 us
  matrix products: 5.2 us -> 0 us
    pallas_call x0 -> x1, Pallas kernels: none -> 23.5 us  [body(): pl.pallas_call(functools.partial(kernel, n, page_len), out_shape=(jax.Sha...]
    select_n x3 -> x0, other arithmetic: 10.6 us -> none  [the longest x1 9.98 us: body(): fresh_pages = jnp.zeros((2, head_dev, fresh_total * page_len, head_size),...]
    all_gather x1 -> x0, waiting for transfers between devices: 9.69 us -> none  [body(): lax.all_gather(tokens, 'tp', axis=0, tiled=True)]
    reduce_scatter x1 -> x0, waiting for transfers between devices: 9 us -> none  [body(): lax.psum_scatter(jnp.dot(contexts, out_weight, preferred_element_type=jnp...]
    reduce_sum x7 -> x0, other arithmetic: 5.82 us -> none  [the longest x1 1.65 us: layer_norm(): spread = jnp.mean(center * center, axis=-1, keepdims=True)]
    dot_general x3 -> x0, matrix products: 5.2 us -> none  [the longest x1 3.06 us: body(): jnp.dot(contexts, out_weight, preferred_element_type=jnp.float32)]
    scatter x2 -> x0, local copies, waits for them, and re-layouts: 5.15 us -> none  [the longest x1 4.42 us: body(): fresh_pages = jnp.zeros((2, head_dev, fresh_total * page_len, head_size),...]
    slice x4 -> x0, local copies, waits for them, and re-layouts: 1.98 us -> none  [the longest x1 1.74 us: body(): cache_pool[1, 0].reshape(-1, head_size)]
  transfers between devices with their start and end apart: 2 -> 0, of which waited for: 2 -> 0; matrix products, arithmetic and copies ran while one was open for 39% -> 0% of each run, Pallas kernels for 0% -> 0%
where the time goes in v1:
time: 29 us; the launch traced here: 28.7 us
  Pallas kernels  23.5 us (81%)
  local copies, waits for them, and re-layouts  4.55 us (16%)
  between operations  0.64 us (2%)
    pallas_call x1, Pallas kernels, body(): pl.pallas_call(functools.partial(kernel, n, page_len), out_shape=(jax.Sha...  23.5 us
    unnamed x2, local copies, waits for them, and re-layouts  3.24 us
    reshape x1, local copies, waits for them, and re-layouts, body(): norm_gain.reshape(1, -1)  1.31 us

profile of v1, /device:TPU:0, one launch (start us, length us, event | category | flops | bytes accessed | tf_op | source)
XLA Modules:
  0.0 28.7 jit_solution(10499028945130055760)
XLA Ops:
  0.6 1.3 %reshape.25.gain_ref = bf16[1,4096]{1,0:T(2,128)(2,1)} reshape(bf16[4096]{0:T(1024)(128)(2,1)} %param.10) | data formatting | bytes 16384 | tf_op jit(solution)/shard_map/reshape | solution.py:356
  1.9 23.5 %shard_map.104 = (bf16[32,4096]{1,0:T(8,128)(2,1)}, bf16[2,256,128]{2,1,0:T(8,128)(2,1)}) custom-call(bf16[32,4096]{1,0:T(8,128)(2,1)} %tok_ref.1, bf16[1,4096]{1,0:T(2,128)(2,1)} %reshape.25.gain_ref, s32[1,128]{1,0:T(1,128)} %bitcast.10, s32[1,8]{1,0:T(1,128)} %bitcast.11, s32[1,48]{1,0:T(1,128)} %bitcast.12, s32[1,16]{1,0:T(1,128)} %bitcast.13, ...), custom_call_target="tpu_custom_call" | custom-call | tf_op jit(solution)/shard_map/pallas_call | solution.py:317
  25.5 1.7 %copy.14 = bf16[32,4096]{1,0:T(8,128)(2,1)} copy(bf16[32,4096]{1,0:T(8,128)(2,1)} %get-tuple-element.10) | data formatting | bytes 524288
  27.2 1.6 %copy.15 = bf16[2,1,16,16,128]{4,3,2,1,0:T(8,128)(2,1)} copy(bf16[2,1,16,16,128]{4,3,2,1,0:T(8,128)(2,1)} %bitcast.9) | data formatting | bytes 262144

commit v2 on v1

--- a/solution.py
+++ b/solution.py
@@ -26,17 +26,23 @@
 def kernel(
     n,
     page_len,
+    tok_hbm,
+    gain_hbm,
+    seg_hbm,
+    prefix_hbm,
+    order_hbm,
+    fresh_hbm,
+    w_hbm,
+    wo_hbm,
+    cache_hbm,
+    out_ref,
+    pages_ref,
     tok_ref,
     gain_ref,
     seg_ref,
     prefix_ref,
     order_ref,
     fresh_ref,
-    w_hbm,
-    wo_hbm,
-    cache_hbm,
-    out_ref,
-    pages_ref,
     xg,
     w_v,
     wo_v,
@@ -48,6 +54,7 @@
     stage,
     land,
     own_sum,
+    in_sem,
     w_sem,
     wo_sem,
     cache_sem,
@@ -77,6 +84,12 @@
     def at_rows(owner):
         return pl.ds(pl.multiple_of(owner * rows, rows), rows)
 
+    small_in = [tok_hbm, gain_hbm, seg_hbm, prefix_hbm, order_hbm, fresh_hbm]
+    small_v = [tok_ref, gain_ref, seg_ref, prefix_ref, order_ref, fresh_ref]
+    small_copies = [
+        pltpu.make_async_copy(source, target, in_sem.at[i])
+        for i, (source, target) in enumerate(zip(small_in, small_v))
+    ]
     cache_copy = pltpu.make_async_copy(cache_hbm, cache_v, cache_sem)
     wo_copy = pltpu.make_async_copy(wo_hbm, wo_v.at[pl.ds(0, head)], wo_sem)
     w_copies = [
@@ -135,16 +148,20 @@
             device_id_type=pl.DeviceIdType.MESH,
         )
 
+    for copy in small_copies[:2]:
+        copy.start()
     barrier = pltpu.get_barrier_semaphore()
     for other in [sibling] + [peer(d) for d in range(1, m)]:
         pl.semaphore_signal(
             barrier, inc=1, device_id={"tp": other}, device_id_type=pl.DeviceIdType.MESH
         )
-    for copy in w_copies:
+    for copy in w_copies + small_copies[2:]:
         copy.start()
     cache_copy.start()
     wo_copy.start()
 
+    for copy in small_copies[:2]:
+        copy.wait()
     values = tok_ref[...].astype(F32)
     mean = jnp.sum(values, axis=1, keepdims=True) * (1.0 / width)
     center = values - mean
@@ -153,13 +170,15 @@
     pl.semaphore_wait(barrier, m)
     for j in range(K_PARTS):
         part = slice(j * kc, (j + 1) * kc)
-        piece = (tok_ref[:, part].astype(F32) - mean) * scale * gain_ref[:, part].astype(F32)
+        piece = (tok_ref[:, part].astype(F32) - mean) * scale * gain_ref[part].reshape(1, kc).astype(F32)
         xg[j, at_rows(me), :] = piece.astype(BF16)
         for d in range(1, m):
             cross(j, d).start()
         forward(j, 0).start()
     wo_push.start()
 
+    for copy in small_copies[2:]:
+        copy.wait()
     seqs = prefix_ref.shape[1]
     seg_row = seg_ref[...].astype(F32)
     prefix_row = prefix_ref[...].astype(F32)
@@ -317,12 +336,18 @@
     attn_out, fresh_pages = pl.pallas_call(
         functools.partial(kernel, n, page_len),
         out_shape=(
-            jax.ShapeDtypeStruct((rows, width), BF16),
-            jax.ShapeDtypeStruct((2, fresh_total * page_len, head), BF16),
+            pltpu.VMEM((rows, width), BF16),
+            pltpu.VMEM((2, fresh_total * page_len, head), BF16),
         ),
-        in_specs=[vmem] * 6 + [hbm] * 3,
+        in_specs=[hbm] * 9,
         out_specs=(vmem, vmem),
         scratch_shapes=[
+            pltpu.VMEM((rows, width), BF16),
+            pltpu.VMEM((width,), BF16),
+            pltpu.VMEM((1, toks), jnp.int32),
+            pltpu.VMEM((1, prefix_pages.shape[0]), jnp.int32),
+            pltpu.VMEM((1, pages), jnp.int32),
+            pltpu.VMEM((1, fresh_total), jnp.int32),
             pltpu.VMEM((K_PARTS, toks, kc), BF16),
             pltpu.VMEM((width, 3 * head), BF16),
             pltpu.VMEM((2 * head, width), BF16),
@@ -334,6 +359,7 @@
             pltpu.VMEM((m - 1, N_PARTS, rows, nc), BF16),
             pltpu.VMEM((m - 1, N_PARTS, rows, nc), BF16),
             pltpu.VMEM((rows, width), F32),
+            dma((6,)),
             dma((K_PARTS,)),
             dma,
             dma,
@@ -353,7 +379,7 @@
         ),
     )(
         tokens,
-        norm_gain.reshape(1, -1),
+        norm_gain,
         segment_ids.reshape(1, -1),
         prefix_pages.reshape(1, -1),
         page_order.reshape(1, -1),

time: 29 us -> 24 us (0.83)
  local copies, waits for them, and re-layouts: 4.55 us -> 1.36 us
  Pallas kernels: 23.5 us -> 21.9 us
    unnamed x2, local copies, waits for them, and re-layouts: 3.24 us -> 1.36 us
    pallas_call x1, Pallas kernels: 23.5 us -> 21.9 us  [body(): pl.pallas_call(functools.partial(kernel, n, page_len), out_shape=(pltpu.V...]
    reshape x1 -> x0, local copies, waits for them, and re-layouts: 1.31 us -> none  [body(): norm_gain.reshape(1, -1)]
where the time goes in v2:
time: 24 us; the launch traced here: 23.9 us
  Pallas kernels  21.9 us (91%)
  local copies, waits for them, and re-layouts  1.36 us (6%)
  between operations  0.64 us (3%)
    pallas_call x1, Pallas kernels, body(): pl.pallas_call(functools.partial(kernel, n, page_len), out_shape=(pltpu.V...  21.9 us
    unnamed x2, local copies, waits for them, and re-layouts  1.36 us

profile of v2, /device:TPU:0, one launch (start us, length us, event | category | flops | bytes accessed | tf_op | source)
XLA Modules:
  0.0 23.9 jit_solution(8325962246867851495)
XLA Ops:
  0.6 21.9 %shard_map.104 = (bf16[32,4096]{1,0:T(8,128)(2,1)S(1)}, bf16[2,256,128]{2,1,0:T(8,128)(2,1)S(1)}) custom-call(bf16[32,4096]{1,0:T(8,128)(2,1)} %tok_hbm.1, bf16[4096]{0:T(1024)(128)(2,1)} %gain_hbm.1, s32[1,128]{1,0:T(1,128)} %bitcast.10, s32[1,8]{1,0:T(1,128)} %bitcast.11, s32[1,48]{1,0:T(1,128)} %bitcast.12, s32[1,16]{1,0:T(1,128)} %bitcast.13, ...), custom_call_target="tpu_custom_call" | custom-call | tf_op jit(solution)/shard_map/pallas_call | solution.py:336
  22.5 0.7 %copy.14 = bf16[32,4096]{1,0:T(8,128)(2,1)} copy(bf16[32,4096]{1,0:T(8,128)(2,1)S(1)} %get-tuple-element.8) | data formatting | bytes 524288
  23.2 0.7 %copy.15 = bf16[2,1,16,16,128]{4,3,2,1,0:T(8,128)(2,1)} copy(bf16[2,1,16,16,128]{4,3,2,1,0:T(8,128)(2,1)S(1)} %bitcast.8) | data formatting | bytes 262144

commit v3 on v2

--- a/solution.py
+++ b/solution.py
@@ -7,7 +7,7 @@
 from jax.sharding import PartitionSpec as P
 
 MODEL_HEADS = 32
-K_PARTS = 8
+K_PARTS = 4
 N_PARTS = 8
 F32 = jnp.float32
 BF16 = jnp.bfloat16
@@ -311,6 +311,17 @@
             give(j, d).wait_send()
 
 
+def write_out(attn_v, pages_v, attn_hbm, pages_hbm, sem):
+    copies = [
+        pltpu.make_async_copy(attn_v, attn_hbm, sem.at[0]),
+        pltpu.make_async_copy(pages_v, pages_hbm, sem.at[1]),
+    ]
+    for copy in copies:
+        copy.start()
+    for copy in copies:
+        copy.wait()
+
+
 def body(
     tokens,
     norm_gain,
@@ -388,6 +399,19 @@
         out_weight,
         cache_pool.reshape(2, cached, head),
     )
+    attn_out, fresh_pages = pl.pallas_call(
+        write_out,
+        out_shape=(
+            jax.ShapeDtypeStruct(attn_out.shape, BF16),
+            jax.ShapeDtypeStruct(fresh_pages.shape, BF16),
+        ),
+        in_specs=[vmem] * 2,
+        out_specs=(hbm, hbm),
+        scratch_shapes=[dma((2,))],
+    )(
+        pltpu.with_memory_space_constraint(attn_out, pltpu.VMEM),
+        pltpu.with_memory_space_constraint(fresh_pages, pltpu.VMEM),
+    )
     return attn_out, fresh_pages.reshape(2, head_dev, fresh_total, page_len, head)
 
 

time: 24 us -> 22.6 us (0.942)
  local copies, waits for them, and re-layouts: 1.36 us -> 0 us
    unnamed x2 -> x0, local copies, waits for them, and re-layouts: 1.36 us -> none
    pallas_call x1, Pallas kernels: 21.9 us -> 21 us  [body(): pl.pallas_call(functools.partial(kernel, n, page_len), out_shape=(pltpu.V...]
    pallas_call x0 -> x1, Pallas kernels: none -> 0.76 us  [body(): pl.pallas_call(write_out, out_shape=(jax.ShapeDtypeStruct(attn_out.shape,...]
where the time goes in v3:
time: 22.6 us; the launch traced here: 22.4 us
  Pallas kernels  21.8 us (96%)
  between operations  0.64 us (3%)
    pallas_call x1, Pallas kernels, body(): pl.pallas_call(functools.partial(kernel, n, page_len), out_shape=(pltpu.V...  21 us
    pallas_call x1, Pallas kernels, body(): pl.pallas_call(write_out, out_shape=(jax.ShapeDtypeStruct(attn_out.shape,...  0.76 us

profile of v3, /device:TPU:0, one launch (start us, length us, event | category | flops | bytes accessed | tf_op | source)
XLA Modules:
  0.0 22.4 jit_solution(7156607203288552581)
XLA Ops:
  0.6 21.0 %shard_map.104 = (bf16[32,4096]{1,0:T(8,128)(2,1)S(1)}, bf16[2,256,128]{2,1,0:T(8,128)(2,1)S(1)}) custom-call(bf16[32,4096]{1,0:T(8,128)(2,1)} %tok_hbm.1, bf16[4096]{0:T(1024)(128)(2,1)} %gain_hbm.1, s32[1,128]{1,0:T(1,128)} %bitcast.9, s32[1,8]{1,0:T(1,128)} %bitcast.10, s32[1,48]{1,0:T(1,128)} %bitcast.11, s32[1,16]{1,0:T(1,128)} %bitcast.12, ...), custom_call_target="tpu_custom_call" | custom-call | tf_op jit(solution)/shard_map/pallas_call | solution.py:347
  21.7 0.8 %shard_map.105 = (bf16[32,4096]{1,0:T(8,128)(2,1)}, bf16[2,256,128]{2,1,0:T(8,128)(2,1)}) custom-call(bf16[32,4096]{1,0:T(8,128)(2,1)S(1)} %get-tuple-element.6.attn_v, bf16[2,256,128]{2,1,0:T(8,128)(2,1)S(1)} %get-tuple-element.7.pages_v), custom_call_target="tpu_custom_call" | custom-call | tf_op jit(solution)/shard_map/pallas_call | solution.py:402
